TPU v7x, 32 devices: a whole 2x2x4 slice. The times are simulated.
32 devices in a mesh: leaf: 32 (over z, y, x, core).
Axes of the slice: x: 2, y: 2, z: 4, core: 2. Of those that a mesh axis runs over, the one named last changes fastest.
Arguments:
- charges: bfloat16 [8192, 128, 128], P('leaf'), may hold values from -6 to 6
- basis_in: bfloat16 [8192, 64, 128], P('leaf'), may hold values from -0.5 to 0.5
- basis_out: bfloat16 [8192, 64, 128], P('leaf'), may hold values from -0.75 to 0.75
- transfer: bfloat16 [1024, 8, 64, 64], P('leaf'), may hold values from -0.375 to 0.375
- leaf_coupling: bfloat16 [16, 64, 64], replicated, may hold values from -0.25 to 0.25
- parent_coupling: bfloat16 [16, 64, 64], replicated, may hold values from -0.25 to 0.25
- leaf_sources: int32 [8192, 16], P('leaf'), may hold values from 0 to 511, as said below
- leaf_counts: int32 [8192], P('leaf'), may hold values from 2 to 16
- leaf_sends: int32 [32, 2, 128], replicated, may hold values from 0 to 255, as said below
- parent_sources: int32 [1024, 16], P('leaf'), may hold values from 0 to 63, as said below
- parent_counts: int32 [1024], P('leaf'), may hold values from 12 to 16
- parent_sends: int32 [32, 32], replicated, may hold values from 0 to 31
Outputs:
- potential: bfloat16 [8192, 128, 128], P('leaf')
Inputs may be any that keep to these rules, and one draw needn't show every extreme that they name: `leaf_sources`: every row of a device's leaf pool is read by some used slot of that device's leaf lists. `leaf_sends`: the 128 leaves offered in one direction are distinct. `parent_sources`: every row of a device's parent pool is read by some used slot of that device's parent lists.
All inputs are finite; a program needn't handle non-finite values.
Results may differ from a plain program's by a relative error of at most 0.007.
Values may be sent and summed in bfloat16 or wider, within the bound.
A program may use at most 256 MiB of HBM per device.

v0:
```python
import math

import jax
import jax.numpy as jnp
from jax import lax
from jax.sharding import PartitionSpec as P


def extended_2(value, sides, width):
    for axis, dim in sides:
        size, length = (lax.axis_size(axis), value.shape[dim])
        up = [(i, (i + 1) % size) for i in range(size - 1)]
        down = [(j, i) for i, j in up]
        last = lax.slice_in_dim(value, length - width, length, axis=dim)
        first = lax.slice_in_dim(value, 0, width, axis=dim)
        before = lax.ppermute(last, axis, up)
        after = lax.ppermute(first, axis, down)
        value = jnp.concatenate([before, value, after], axis=dim)
    return value


def pooled_product(pool_rows, sources, counts, coupling):
    target_rows, list_width = sources.shape
    rank_width = coupling.shape[1]
    rhs_width = pool_rows.shape[-1]
    pool_size = pool_rows.shape[0]
    extended = jnp.concatenate(
        [pool_rows, jnp.zeros((1, rank_width, rhs_width), pool_rows.dtype)], 0
    )
    stacked = jnp.transpose(coupling, (1, 0, 2)).reshape(rank_width, list_width * rank_width)
    block_rows = math.gcd(target_rows, 32)
    blocks = target_rows // block_rows

    def one_block(pieces):
        picked_rows, limits = pieces
        valid_mask = lax.broadcasted_iota(jnp.int32, picked_rows.shape, 1) < limits[:, None]
        redirected = jnp.where(valid_mask, picked_rows, pool_size)
        gathered = extended[redirected]
        flattened = gathered.reshape(block_rows, list_width * rank_width, rhs_width)
        return jnp.einsum("ac,tcr->tar", stacked, flattened, preferred_element_type=jnp.float32)

    fields = lax.map(
        one_block,
        (sources.reshape(blocks, block_rows, list_width), counts.reshape(blocks, block_rows)),
    )
    return fields.reshape(target_rows, rank_width, rhs_width)


def shards(
    charges,
    basis_in,
    basis_out,
    transfer,
    leaf_coupling,
    parent_coupling,
    leaf_sources,
    leaf_counts,
    leaf_sends,
    parent_sources,
    parent_counts,
    parent_sends,
):
    per_dev = charges.shape[0]
    rank_width = basis_in.shape[1]
    rhs_width = charges.shape[2]
    parent_rows = transfer.shape[0]
    count_dev = lax.axis_size("leaf")
    own_index = lax.axis_index("leaf")
    up_leaf = jnp.einsum(
        "nkp,npr->nkr", basis_in, charges, preferred_element_type=jnp.float32
    ).astype(jnp.bfloat16)
    left_dev = jnp.maximum(own_index - 1, 0)
    right_dev = jnp.minimum(own_index + 1, count_dev - 1)
    padded = extended_2(up_leaf, (("leaf", 0),), per_dev)
    left_list = lax.dynamic_index_in_dim(leaf_sends, left_dev, 0, keepdims=False)[1]
    right_list = lax.dynamic_index_in_dim(leaf_sends, right_dev, 0, keepdims=False)[0]
    from_left = padded[:per_dev][left_list]
    from_right = padded[2 * per_dev :][right_list]
    leaf_rows_pool = jnp.concatenate([up_leaf, from_left, from_right], 0)
    leaf_field = pooled_product(leaf_rows_pool, leaf_sources, leaf_counts, leaf_coupling)
    grouped = up_leaf.reshape(parent_rows, 8, rank_width, rhs_width)
    up_parent = jnp.einsum(
        "pcab,pcar->pbr", transfer, grouped, preferred_element_type=jnp.float32
    ).astype(jnp.bfloat16)
    own_row = lax.dynamic_index_in_dim(parent_sends, own_index, 0, keepdims=False)
    arrived = lax.all_to_all(up_parent[own_row], "leaf", split_axis=0, concat_axis=0, tiled=True)
    parent_rows_pool = jnp.concatenate([up_parent, arrived], 0)
    parent_field = pooled_product(parent_rows_pool, parent_sources, parent_counts, parent_coupling)
    parent_down = parent_field.astype(jnp.bfloat16)
    pushed = jnp.einsum("pcab,pbr->pcar", transfer, parent_down, preferred_element_type=jnp.float32)
    leaf_total = (leaf_field + pushed.reshape(per_dev, rank_width, rhs_width)).astype(jnp.bfloat16)
    return jnp.einsum(
        "nkp,nkr->npr", basis_out, leaf_total, preferred_element_type=jnp.float32
    ).astype(jnp.bfloat16)


def solution(mesh):
    return jax.shard_map(
        shards,
        mesh=mesh,
        in_specs=(
            P("leaf", None, None),
            P("leaf", None, None),
            P("leaf", None, None),
            P("leaf", None, None, None),
            P(),
            P(),
            P("leaf", None),
            P("leaf"),
            P(),
            P("leaf", None),
            P("leaf"),
            P(),
        ),
        out_specs=P("leaf", None, None),
        check_vma=False,
    )
```

profile of v0, /device:TPU:1, one launch (start us, length us, event | category | flops | bytes accessed | tf_op | source)
XLA Modules:
  0.0 407.5 jit_solution(15319406426279353346)
XLA Ops:
  0.0 9.0 %convolution_convert_fusion = bf16[256,64,128]{2,1,0:T(8,128)(2,1)} fusion(bf16[256,64,128]{2,1,0:T(8,128)(2,1)} %param.15, bf16[256,128,128]{2,1,0:T(8,128)(2,1)} %param.14), kind=kOutput, calls=%fused_computation.18 | convolution fusion | flops 538968064 | bytes 16777216 | tf_op jit(solution)/shard_map/nkp,npr->nkr/dot_general | solution.py:69
  9.0 4.5 %collective-permute-start = (bf16[256,64,128]{2,1,0:T(8,128)(2,1)}, bf16[256,64,128]{2,1,0:T(8,128)(2,1)}, u32[]{:S(2)}, u32[]{:S(2)}) collective-permute-start(bf16[256,64,128]{2,1,0:T(8,128)(2,1)} %convolution_convert_fusion), channel_id=1, source_target_pairs={{0,1},{1,2},{2,3},{3,4},{4,5},{5,6},{6,7},{7,8},{8,9},{9,10},{10,1... | collective-permute-start | bytes 12582920 | tf_op jit(solution)/shard_map/ppermute | solution.py:16
  13.5 1.9 collective-permute-start.1
  15.4 0.7 fusion.14
  16.1 0.0 copy-start.2
  16.1 0.0 copy-start.3
  16.2 0.0 copy-start.5
  16.2 0.0 copy-start.4
  16.2 0.0 copy-start.6
  16.2 5.1 %fusion.8 = bf16[32,64,128]{2,1,0:T(8,128)(2,1)S(1)} fusion(bf16[32,8,64,128]{3,2,1,0:T(8,128)(2,1)} %bitcast.13, bf16[32,8,64,64]{3,2,1,0:T(8,128)(2,1)} %param.17), kind=kOutput, calls=%fused_computation.25 | convolution fusion | flops 268697600 | bytes 6815744 | tf_op jit(solution)/shard_map/pcab,pcar->pbr/dot_general | solution.py:82
  21.3 1.4 gather_fusion.3
  22.7 6.6 %all-to-all-start = ((bf16[32,64,128]{2,1,0:T(8,128)(2,1)}), bf16[32,64,128]{2,1,0:T(8,128)(2,1)S(1)}, u32[]{:S(2)}, u32[]{:S(2)}) async-start(bf16[32,64,128]{2,1,0:T(8,128)(2,1)} %gather_fusion.3), calls=%async_computation | async-start | bytes 1048576 | tf_op jit(solution)/shard_map/all_to_all | solution.py:86
  29.3 0.2 copy.16
  29.4 0.2 reshape.190
  29.7 0.1 copy.25
  29.8 0.1 reshape.188
  29.9 0.1 copy.19
  29.9 0.1 reshape.228
  30.0 0.7 constant_dynamic-slice_fusion.3
  30.8 80.4 %all-to-all-done = bf16[32,64,128]{2,1,0:T(8,128)(2,1)S(1)} async-done(((bf16[32,64,128]{2,1,0:T(8,128)(2,1)}), bf16[32,64,128]{2,1,0:T(8,128)(2,1)S(1)}, u32[]{:S(2)}, u32[]{:S(2)}) %all-to-all-start) | async-done | bytes 524320 | tf_op jit(solution)/shard_map/all_to_all | solution.py:86
  111.2 0.1 pad_maximum_fusion.1
  111.3 13.5 %gather_fusion.4 = bf16[512,64,128]{2,1,0:T(8,128)(2,1)} fusion(bf16[65,64,128]{2,1,0:T(8,128)(2,1)S(1)} %pad_maximum_fusion.1, s32[1024]{0:T(1024)S(1)} %pad_clamp_fusion.1), kind=kCustom, calls=%fused_computation.4 | custom fusion | bytes 16779264 | tf_op jit(solution)/shard_map/while/body/eval_jaxpr/gather | solution.py:38
  124.8 10.5 %fusion.7 = f32[32,128,8,64]{1,3,2,0:T(8,128)} fusion(bf16[32,8,64,64]{3,2,1,0:T(8,128)(2,1)} %param.17, bf16[32,16,64,128]{3,2,1,0:T(8,128)(2,1)} %bitcast.100, bf16[16,64,64]{2,1,0:T(8,128)(2,1)S(1)} %copy-done), kind=kOutput, calls=%fused_computation.24 | convolution fusion | flops 805568512 | bytes 19005440 | tf_op jit(solution)/shard_map/pcab,pbr->pcar/dot_general | solution.py:90
  135.3 0.0 collective-permute-done
  135.3 3.1 gather_fusion.1
  138.5 0.0 collective-permute-done.1
  138.5 4.3 %gather_fusion.2 = bf16[128,64,128]{2,1,0:T(8,128)(2,1)} fusion(bf16[256,64,128]{2,1,0:T(8,128)(2,1)} %collective-permute-done.1, s32[1024]{0:T(1024)S(1)} %pad_clamp_fusion.3), kind=kCustom, calls=%fused_computation.2 | custom fusion | bytes 4194816 | tf_op jit(solution)/shard_map/gather | solution.py:78
  142.8 7.0 %pad_maximum_fusion = bf16[513,64,128]{2,1,0:T(8,128)(2,1)} fusion(bf16[1,64,128]{2,1,0:T(8,128)(2,1)S(1)} %broadcast.119, bf16[128,64,128]{2,1,0:T(8,128)(2,1)} %gather_fusion.2, bf16[128,64,128]{2,1,0:T(8,128)(2,1)S(1)} %gather_fusion.1, bf16[256,64,128]{2,1,0:T(8,128)(2,1)} %convolution_convert_fusion), kind=kLoop, calls=%fused_computation.14 | loop fusion | flops 12607488 | bytes 16809984 | tf_op jit(solution)/shard_map/concatenate | solution.py:27
  149.8 229.9 %while.2 = (s32[]{:T(128)}, f32[8,32,64,128]{3,2,1,0:T(8,128)}, s32[8,32]{1,0:T(8,128)S(1)}, s32[8,32,16]{2,1,0:T(8,128)S(1)}, bf16[513,64,128]{2,1,0:T(8,128)(2,1)}, /*index=5*/bf16[64,1024]{1,0:T(8,128)(2,1)S(1)}, s32[]{:T(128)}) while((s32[]{:T(128)}, f32[8,32,64,128]{3,2,1,0:T(8,128)}, s32[8,32]{1,0:T(8,128)S(1)}, ...), condition=%wide.region_1.2_spmd, body=%wide.region_0.1_spmd.sunk | while | flops 536874496 | bytes 26362836 | solution.py:42
  149.8 0.1 compare_select_fusion.6
  149.9 0.1 reshape.248
  150.0 22.6 %gather_fusion = bf16[512,64,128]{2,1,0:T(8,128)(2,1)} fusion(bf16[513,64,128]{2,1,0:T(8,128)(2,1)} %get-tuple-element.131, s32[1024]{0:T(1024)S(1)} %pad_clamp_fusion.6), kind=kCustom, calls=%fused_computation.clone.1 | custom fusion | bytes 16779264 | tf_op jit(solution)/shard_map/while/body/eval_jaxpr/gather | solution.py:38
  172.6 5.9 %fusion.31 = f32[8,32,64,128]{3,2,1,0:T(8,128)} fusion(f32[8,32,64,128]{3,2,1,0:T(8,128)} %get-tuple-element.121, s32[]{:T(128)} %get-tuple-element.120, bf16[32,1024,128]{2,1,0:T(8,128)(2,1)} %bitcast.99, bf16[64,1024]{1,0:T(8,128)(2,1)S(1)} %get-tuple-element.132), kind=kOutput, calls=%fused_computation.6.clone.1 | convolution fusion | flops 536870912 | bytes 9568768 | tf_op jit(solution)/shard_map/while/body/eval_jaxpr/ac,tcr->tar/dot_general | solution.py:40
  178.6 0.1 compare_select_fusion.6
  178.6 0.1 reshape.248
  178.7 22.6 %gather_fusion = bf16[512,64,128]{2,1,0:T(8,128)(2,1)} fusion(bf16[513,64,128]{2,1,0:T(8,128)(2,1)} %get-tuple-element.131, s32[1024]{0:T(1024)S(1)} %pad_clamp_fusion.6), kind=kCustom, calls=%fused_computation.clone.1 | custom fusion | bytes 16779264 | tf_op jit(solution)/shard_map/while/body/eval_jaxpr/gather | solution.py:38
  201.4 5.9 %fusion.31 = f32[8,32,64,128]{3,2,1,0:T(8,128)} fusion(f32[8,32,64,128]{3,2,1,0:T(8,128)} %get-tuple-element.121, s32[]{:T(128)} %get-tuple-element.120, bf16[32,1024,128]{2,1,0:T(8,128)(2,1)} %bitcast.99, bf16[64,1024]{1,0:T(8,128)(2,1)S(1)} %get-tuple-element.132), kind=kOutput, calls=%fused_computation.6.clone.1 | convolution fusion | flops 536870912 | bytes 9568768 | tf_op jit(solution)/shard_map/while/body/eval_jaxpr/ac,tcr->tar/dot_general | solution.py:40
  207.3 0.1 compare_select_fusion.6
  207.4 0.1 reshape.248
  207.5 22.6 %gather_fusion = bf16[512,64,128]{2,1,0:T(8,128)(2,1)} fusion(bf16[513,64,128]{2,1,0:T(8,128)(2,1)} %get-tuple-element.131, s32[1024]{0:T(1024)S(1)} %pad_clamp_fusion.6), kind=kCustom, calls=%fused_computation.clone.1 | custom fusion | bytes 16779264 | tf_op jit(solution)/shard_map/while/body/eval_jaxpr/gather | solution.py:38
  230.1 5.9 %fusion.31 = f32[8,32,64,128]{3,2,1,0:T(8,128)} fusion(f32[8,32,64,128]{3,2,1,0:T(8,128)} %get-tuple-element.121, s32[]{:T(128)} %get-tuple-element.120, bf16[32,1024,128]{2,1,0:T(8,128)(2,1)} %bitcast.99, bf16[64,1024]{1,0:T(8,128)(2,1)S(1)} %get-tuple-element.132), kind=kOutput, calls=%fused_computation.6.clone.1 | convolution fusion | flops 536870912 | bytes 9568768 | tf_op jit(solution)/shard_map/while/body/eval_jaxpr/ac,tcr->tar/dot_general | solution.py:40
  236.0 0.1 compare_select_fusion.6
  236.1 0.1 reshape.248
  236.2 22.6 %gather_fusion = bf16[512,64,128]{2,1,0:T(8,128)(2,1)} fusion(bf16[513,64,128]{2,1,0:T(8,128)(2,1)} %get-tuple-element.131, s32[1024]{0:T(1024)S(1)} %pad_clamp_fusion.6), kind=kCustom, calls=%fused_computation.clone.1 | custom fusion | bytes 16779264 | tf_op jit(solution)/shard_map/while/body/eval_jaxpr/gather | solution.py:38
  258.8 5.9 %fusion.31 = f32[8,32,64,128]{3,2,1,0:T(8,128)} fusion(f32[8,32,64,128]{3,2,1,0:T(8,128)} %get-tuple-element.121, s32[]{:T(128)} %get-tuple-element.120, bf16[32,1024,128]{2,1,0:T(8,128)(2,1)} %bitcast.99, bf16[64,1024]{1,0:T(8,128)(2,1)S(1)} %get-tuple-element.132), kind=kOutput, calls=%fused_computation.6.clone.1 | convolution fusion | flops 536870912 | bytes 9568768 | tf_op jit(solution)/shard_map/while/body/eval_jaxpr/ac,tcr->tar/dot_general | solution.py:40
  264.8 0.1 compare_select_fusion.6
  264.9 0.1 reshape.248
  265.0 22.6 %gather_fusion = bf16[512,64,128]{2,1,0:T(8,128)(2,1)} fusion(bf16[513,64,128]{2,1,0:T(8,128)(2,1)} %get-tuple-element.131, s32[1024]{0:T(1024)S(1)} %pad_clamp_fusion.6), kind=kCustom, calls=%fused_computation.clone.1 | custom fusion | bytes 16779264 | tf_op jit(solution)/shard_map/while/body/eval_jaxpr/gather | solution.py:38
  287.6 5.9 %fusion.31 = f32[8,32,64,128]{3,2,1,0:T(8,128)} fusion(f32[8,32,64,128]{3,2,1,0:T(8,128)} %get-tuple-element.121, s32[]{:T(128)} %get-tuple-element.120, bf16[32,1024,128]{2,1,0:T(8,128)(2,1)} %bitcast.99, bf16[64,1024]{1,0:T(8,128)(2,1)S(1)} %get-tuple-element.132), kind=kOutput, calls=%fused_computation.6.clone.1 | convolution fusion | flops 536870912 | bytes 9568768 | tf_op jit(solution)/shard_map/while/body/eval_jaxpr/ac,tcr->tar/dot_general | solution.py:40
  293.5 0.1 compare_select_fusion.6
  293.6 0.1 reshape.248
  293.6 22.6 %gather_fusion = bf16[512,64,128]{2,1,0:T(8,128)(2,1)} fusion(bf16[513,64,128]{2,1,0:T(8,128)(2,1)} %get-tuple-element.131, s32[1024]{0:T(1024)S(1)} %pad_clamp_fusion.6), kind=kCustom, calls=%fused_computation.clone.1 | custom fusion | bytes 16779264 | tf_op jit(solution)/shard_map/while/body/eval_jaxpr/gather | solution.py:38
  316.3 6.0 %fusion.31 = f32[8,32,64,128]{3,2,1,0:T(8,128)} fusion(f32[8,32,64,128]{3,2,1,0:T(8,128)} %get-tuple-element.121, s32[]{:T(128)} %get-tuple-element.120, bf16[32,1024,128]{2,1,0:T(8,128)(2,1)} %bitcast.99, bf16[64,1024]{1,0:T(8,128)(2,1)S(1)} %get-tuple-element.132), kind=kOutput, calls=%fused_computation.6.clone.1 | convolution fusion | flops 536870912 | bytes 9568768 | tf_op jit(solution)/shard_map/while/body/eval_jaxpr/ac,tcr->tar/dot_general | solution.py:40
  322.2 0.1 compare_select_fusion.6
  322.3 0.1 reshape.248
  322.4 22.6 %gather_fusion = bf16[512,64,128]{2,1,0:T(8,128)(2,1)} fusion(bf16[513,64,128]{2,1,0:T(8,128)(2,1)} %get-tuple-element.131, s32[1024]{0:T(1024)S(1)} %pad_clamp_fusion.6), kind=kCustom, calls=%fused_computation.clone.1 | custom fusion | bytes 16779264 | tf_op jit(solution)/shard_map/while/body/eval_jaxpr/gather | solution.py:38
  345.0 5.9 %fusion.31 = f32[8,32,64,128]{3,2,1,0:T(8,128)} fusion(f32[8,32,64,128]{3,2,1,0:T(8,128)} %get-tuple-element.121, s32[]{:T(128)} %get-tuple-element.120, bf16[32,1024,128]{2,1,0:T(8,128)(2,1)} %bitcast.99, bf16[64,1024]{1,0:T(8,128)(2,1)S(1)} %get-tuple-element.132), kind=kOutput, calls=%fused_computation.6.clone.1 | convolution fusion | flops 536870912 | bytes 9568768 | tf_op jit(solution)/shard_map/while/body/eval_jaxpr/ac,tcr->tar/dot_general | solution.py:40
  351.0 0.1 compare_select_fusion.6
  351.0 0.1 reshape.248
  351.1 22.6 %gather_fusion = bf16[512,64,128]{2,1,0:T(8,128)(2,1)} fusion(bf16[513,64,128]{2,1,0:T(8,128)(2,1)} %get-tuple-element.131, s32[1024]{0:T(1024)S(1)} %pad_clamp_fusion.6), kind=kCustom, calls=%fused_computation.clone.1 | custom fusion | bytes 16779264 | tf_op jit(solution)/shard_map/while/body/eval_jaxpr/gather | solution.py:38
  373.8 6.0 %fusion.31 = f32[8,32,64,128]{3,2,1,0:T(8,128)} fusion(f32[8,32,64,128]{3,2,1,0:T(8,128)} %get-tuple-element.121, s32[]{:T(128)} %get-tuple-element.120, bf16[32,1024,128]{2,1,0:T(8,128)(2,1)} %bitcast.99, bf16[64,1024]{1,0:T(8,128)(2,1)S(1)} %get-tuple-element.132), kind=kOutput, calls=%fused_computation.6.clone.1 | convolution fusion | flops 536870912 | bytes 9568768 | tf_op jit(solution)/shard_map/while/body/eval_jaxpr/ac,tcr->tar/dot_general | solution.py:40
  379.7 7.9 %fusion.3 = bf16[256,64,128]{2,1,0:T(8,128)(2,1)S(1)} fusion(f32[32,128,8,64]{1,3,2,0:T(8,128)} %fusion.7, f32[8,32,64,128]{3,2,1,0:T(8,128)} %get-tuple-element.55), kind=kLoop, calls=%fused_computation.16 | loop fusion | flops 4194304 | bytes 20971520 | tf_op jit(solution)/shard_map/convert_element_type | solution.py:91
  387.7 7.9 %convert_bitcast_fusion = bf16[256,128,128]{1,2,0:T(8,128)(2,1)} fusion(bf16[256,64,128]{2,1,0:T(8,128)(2,1)S(1)} %fusion.3, bf16[256,64,128]{2,1,0:T(8,128)(2,1)} %param.16), kind=kOutput, calls=%fused_computation.17 | convolution fusion | flops 541065216 | bytes 16777216 | tf_op jit(solution)/shard_map/nkp,nkr->npr/dot_general | solution.py:92
  395.6 12.0 %copy.20 = bf16[256,128,128]{2,1,0:T(8,128)(2,1)} copy(bf16[256,128,128]{1,2,0:T(8,128)(2,1)} %convert_bitcast_fusion) | data formatting | bytes 16777216 | tf_op jit(solution)/shard_map/convert_element_type | solution.py:94
  (34 shorter events, 0.2 us)
Async XLA Ops:
  0.0 124.8 %copy-start = (bf16[16,64,64]{2,1,0:T(8,128)(2,1)S(1)}, bf16[16,64,64]{2,1,0:T(8,128)(2,1)}, u32[]{:S(2)}) copy-start(bf16[16,64,64]{2,1,0:T(8,128)(2,1)} %param.19) | copy-start | bytes 393220
  9.0 126.3 %collective-permute-start = (bf16[256,64,128]{2,1,0:T(8,128)(2,1)}, bf16[256,64,128]{2,1,0:T(8,128)(2,1)}, u32[]{:S(2)}, u32[]{:S(2)}) collective-permute-start(bf16[256,64,128]{2,1,0:T(8,128)(2,1)} %convolution_convert_fusion), channel_id=1, source_target_pairs={{0,1},{1,2},{2,3},{3,4},{4,5},{5,6},{6,7},{7,8},{8,9},{9,10},{10,1... | collective-permute-start | bytes 12582920 | tf_op jit(solution)/shard_map/ppermute | solution.py:16
  13.5 125.0 %collective-permute-start.1 = (bf16[256,64,128]{2,1,0:T(8,128)(2,1)}, bf16[256,64,128]{2,1,0:T(8,128)(2,1)}, u32[]{:S(2)}, u32[]{:S(2)}) collective-permute-start(bf16[256,64,128]{2,1,0:T(8,128)(2,1)} %convolution_convert_fusion), channel_id=1, source_target_pairs={{1,0},{2,1},{3,2},{4,3},{5,4},{6,5},{7,6},{8,7},{9,8},{10,9},{11,1... | collective-permute-start | bytes 12582920 | tf_op jit(solution)/shard_map/ppermute | solution.py:17
  16.1 13.1 %copy-start.2 = (bf16[16,64,64]{2,1,0:T(8,128)(2,1)S(1)}, bf16[16,64,64]{2,1,0:T(8,128)(2,1)}, u32[]{:S(2)}) copy-start(bf16[16,64,64]{2,1,0:T(8,128)(2,1)} %param.18) | copy-start | bytes 393220
  16.1 13.5 %copy-start.3 = (s32[256,16]{0,1:T(8,128)S(1)}, s32[256,16]{0,1:T(8,128)}, u32[]{:S(2)}) copy-start(s32[256,16]{0,1:T(8,128)} %param.20) | copy-start | bytes 49156
  16.2 13.6 %copy-start.5 = (s32[256]{0:T(256)S(1)}, s32[256]{0:T(256)}, u32[]{:S(2)}) copy-start(s32[256]{0:T(256)} %param.21) | copy-start | bytes 3076
  16.2 13.7 %copy-start.4 = (s32[32,16]{0,1:T(8,128)S(1)}, s32[32,16]{0,1:T(8,128)}, u32[]{:S(2)}) copy-start(s32[32,16]{0,1:T(8,128)} %param.23) | copy-start | bytes 6148
  16.2 13.7 %copy-start.6 = (s32[32]{0:T(128)S(1)}, s32[32]{0:T(128)}, u32[]{:S(2)}) copy-start(s32[32]{0:T(128)} %param.24) | copy-start | bytes 388
  22.7 88.5 %all-to-all-start = ((bf16[32,64,128]{2,1,0:T(8,128)(2,1)}), bf16[32,64,128]{2,1,0:T(8,128)(2,1)S(1)}, u32[]{:S(2)}, u32[]{:S(2)}) async-start(bf16[32,64,128]{2,1,0:T(8,128)(2,1)} %gather_fusion.3), calls=%async_computation | async-start | bytes 1048576 | tf_op jit(solution)/shard_map/all_to_all | solution.py:86
  395.6 12.0 %copy-start.1 = (bf16[16,64,64]{2,1,0:T(8,128)(2,1)S(1)}, bf16[16,64,64]{2,1,0:T(8,128)(2,1)}, u32[]{:S(2)}) copy-start(bf16[16,64,64]{2,1,0:T(8,128)(2,1)} %param.19) | copy-start | bytes 393220
where the time goes:
time: 411 us; the launch traced here: 408 us
  local copies, waits for them, and re-layouts  217 us (53%)
  waiting for transfers between devices  80.4 us (20%)
  matrix products  79.9 us (19%)
  other arithmetic  16.5 us (4%)
  starting transfers between devices  13 us (3%)
    gather x9, local copies, waits for them, and re-layouts, one_block(): gathered = extended[redirected]  194 us
    all_to_all x1, waiting for transfers between devices, shards(): lax.all_to_all(up_parent[own_row], 'leaf', split_axis=0, concat_axis=0, t...  80.4 us
    dot_general x8, matrix products, one_block(): jnp.einsum('ac,tcr->tar', stacked, flattened, preferred_element_type=jnp....  47.5 us
    convert_element_type x1, local copies, waits for them, and re-layouts, shards(): return jnp.einsum('nkp,nkr->npr', basis_out, leaf_total, preferred_elemen...  12 us
    dot_general x1, matrix products, shards(): jnp.einsum('pcab,pbr->pcar', transfer, parent_down, preferred_element_typ...  10.5 us
    dot_general x1, matrix products, shards(): jnp.einsum('nkp,npr->nkr', basis_in, charges, preferred_element_type=jnp....  8.99 us
  transfers between devices with their start and end apart: 3, of which 1 were waited for; matrix products, arithmetic and copies ran while one was open for 9% of the time, Pallas kernels for 0%

commit v1 on v0

v1 whole, which is shorter than its diff:
```python
import functools

import jax
import jax.numpy as jnp
from jax import lax
from jax.experimental import pallas as pl
from jax.experimental.pallas import tpu as pltpu
from jax.sharding import PartitionSpec as P

CHUNKS = 4
ANY = pl.BlockSpec(memory_space=pl.ANY)
SMEM = pl.BlockSpec(memory_space=pltpu.SMEM)
CONTRACT_FIRST = (((0,), (0,)), ((), ()))


def upward_kernel(
    n,
    steps,
    charges,
    basis_in,
    transfer,
    leaf_sends,
    parent_sends,
    up_out,
    remote_out,
    parents_out,
    up_all,
    parent_all,
    stage,
    parent_stage,
    zeros,
    send_sem,
    recv_sem,
    parent_send_sem,
    parent_recv_sem,
    local_sem,
):
    me = lax.axis_index("leaf")
    step = pl.program_id(0)
    block = charges.shape[0]
    parents = transfer.shape[0]
    rank, rhs = up_all.shape[1:]
    own_parents = parent_all.shape[0]
    side = stage.shape[1]
    piece = side // CHUNKS

    @pl.when(step == 0)
    def _():
        barrier = pltpu.get_barrier_semaphore()

        def greet(k, carry):
            pl.semaphore_signal(
                barrier,
                inc=1,
                device_id=(lax.rem(me + k, n),),
                device_id_type=pl.DeviceIdType.MESH,
            )
            return carry

        lax.fori_loop(1, n, greet, 0)

    for leaf in range(block):
        row = jnp.dot(basis_in[leaf], charges[leaf], preferred_element_type=jnp.float32).astype(jnp.bfloat16)
        up_out[leaf] = row
        up_all[step * block + leaf] = row
    for p in range(parents):
        children = up_out[8 * p : 8 * p + 8].reshape(8 * rank, rhs)
        parent_all[step * parents + p] = lax.dot_general(
            transfer[p].reshape(8 * rank, rank), children, CONTRACT_FIRST, preferred_element_type=jnp.float32
        ).astype(jnp.bfloat16)

    @pl.when(step == steps - 1)
    def _():
        pl.semaphore_wait(pltpu.get_barrier_semaphore(), n - 1)

        def leaf_copy(direction, c):
            target = me - 1 if direction == 0 else me + 1
            return pltpu.make_async_remote_copy(
                src_ref=stage.at[direction, pl.ds(c * piece, piece)],
                dst_ref=remote_out.at[pl.ds((1 - direction) * side + c * piece, piece)],
                send_sem=send_sem.at[direction, c],
                recv_sem=recv_sem.at[direction, c],
                device_id=(target,),
                device_id_type=pl.DeviceIdType.MESH,
            )

        def zero_copy(half, c):
            return pltpu.make_async_copy(
                zeros, remote_out.at[pl.ds(half * side + c * piece, piece)], local_sem.at[1 + half, c]
            )

        def has_target(direction):
            return me > 0 if direction == 0 else me < n - 1

        for c in range(CHUNKS):
            for direction in range(2):

                def fill(i, carry):
                    stage[direction, c * piece + i] = up_all[leaf_sends[me, direction, c * piece + i]]
                    return carry

                lax.fori_loop(0, piece, fill, 0, unroll=4)

                @pl.when(has_target(direction))
                def _():
                    leaf_copy(direction, c).start()

        def fill_parent(d, carry):
            parent_stage[d] = parent_all[parent_sends[me, d]]
            return carry

        lax.fori_loop(0, n, fill_parent, 0)

        def parent_copy(k):
            target = lax.rem(me + k, n)
            return pltpu.make_async_remote_copy(
                src_ref=parent_stage.at[target],
                dst_ref=parents_out.at[own_parents + me],
                send_sem=parent_send_sem.at[k],
                recv_sem=parent_recv_sem.at[k],
                device_id=(target,),
                device_id_type=pl.DeviceIdType.MESH,
            )

        def start_parent(k, carry):
            parent_copy(k).start()
            return carry

        lax.fori_loop(1, n, start_parent, 0)
        own = [
            pltpu.make_async_copy(parent_all, parents_out.at[pl.ds(0, own_parents)], local_sem.at[0, 0]),
            pltpu.make_async_copy(parent_stage.at[me], parents_out.at[own_parents + me], local_sem.at[0, 1]),
        ]
        for copy in own:
            copy.start()
        zeros[...] = jnp.zeros_like(zeros)
        for half in range(2):

            @pl.when(jnp.logical_not(has_target(half)))
            def _():
                for c in range(CHUNKS):
                    zero_copy(half, c).start()
                for c in range(CHUNKS):
                    zero_copy(half, c).wait()

        for copy in own:
            copy.wait()

        def wait_parent(k, carry):
            source = lax.rem(me - k + n, n)
            copy = pltpu.make_async_remote_copy(
                src_ref=parent_stage.at[lax.rem(me + k, n)],
                dst_ref=parents_out.at[own_parents + source],
                send_sem=parent_send_sem.at[k],
                recv_sem=parent_recv_sem.at[k],
                device_id=(lax.rem(me + k, n),),
                device_id_type=pl.DeviceIdType.MESH,
            )
            copy.wait_send()
            copy.wait_recv()
            return carry

        lax.fori_loop(1, n, wait_parent, 0)
        for c in range(CHUNKS):
            for direction in range(2):

                @pl.when(has_target(direction))
                def _():
                    leaf_copy(direction, c).wait_send()

                @pl.when(has_target(1 - direction))
                def _():
                    leaf_copy(direction, c).wait_recv()


def field_pair(first, second, pool, sources, counts, stacked):
    width = sources.shape[1]
    spare = pool.shape[0] - 1
    columns = []
    for target in (first, second):
        limit = counts[target]
        rows = [pool[jnp.where(j < limit, sources[target, j], spare)] for j in range(width)]
        columns.append(jnp.concatenate(rows, 0))
    return jnp.dot(stacked[...], jnp.concatenate(columns, 1), preferred_element_type=jnp.float32)


def downward_kernel(
    leaf_sources,
    leaf_counts,
    parent_sources,
    parent_counts,
    leaf_coupling,
    parent_coupling,
    up_leaf,
    remote,
    parent_pool,
    transfer,
    basis_out,
    potential,
    pool,
    ppool,
    stacked,
    pstacked,
    down,
    sem,
):
    step = pl.program_id(0)
    block = basis_out.shape[0]
    parents = transfer.shape[0]
    own, rank, rhs = up_leaf.shape
    far = remote.shape[0]
    all_parents = parent_pool.shape[0]

    @pl.when(step == 0)
    def _():
        copies = [
            pltpu.make_async_copy(parent_pool, ppool.at[pl.ds(0, all_parents)], sem.at[0]),
            pltpu.make_async_copy(up_leaf, pool.at[pl.ds(0, own)], sem.at[1]),
            pltpu.make_async_copy(remote, pool.at[pl.ds(own, far)], sem.at[2]),
        ]
        for copy in copies:
            copy.start()
        pool[own + far] = jnp.zeros((rank, rhs), pool.dtype)
        ppool[all_parents] = jnp.zeros((rank, rhs), ppool.dtype)
        for j in range(leaf_coupling.shape[0]):
            stacked[:, j * rank : (j + 1) * rank] = leaf_coupling[j]
        for j in range(parent_coupling.shape[0]):
            pstacked[:, j * rank : (j + 1) * rank] = parent_coupling[j]
        copies[0].wait()

        def parent_pair(i, carry):
            field = field_pair(2 * i, 2 * i + 1, ppool, parent_sources, parent_counts, pstacked)
            down[2 * i] = field[:, :rhs].astype(down.dtype)
            down[2 * i + 1] = field[:, rhs:].astype(down.dtype)
            return carry

        lax.fori_loop(0, down.shape[0] // 2, parent_pair, 0)
        copies[1].wait()
        copies[2].wait()

    for p in range(parents):
        pushed = jnp.dot(
            transfer[p].reshape(8 * rank, rank), down[step * parents + p], preferred_element_type=jnp.float32
        )
        for c in range(0, 8, 2):
            leaf = 8 * p + c
            target = step * block + leaf
            field = field_pair(target, target + 1, pool, leaf_sources, leaf_counts, stacked)
            for k in range(2):
                total = field[:, k * rhs : (k + 1) * rhs] + pushed[(c + k) * rank : (c + k + 1) * rank]
                potential[leaf + k] = lax.dot_general(
                    basis_out[leaf + k],
                    total.astype(jnp.bfloat16),
                    CONTRACT_FIRST,
                    preferred_element_type=jnp.float32,
                ).astype(potential.dtype)


def shards(
    n,
    charges,
    basis_in,
    basis_out,
    transfer,
    leaf_coupling,
    parent_coupling,
    leaf_sources,
    leaf_counts,
    leaf_sends,
    parent_sources,
    parent_counts,
    parent_sends,
):
    leaves, points, rhs = charges.shape
    rank = basis_in.shape[1]
    parents = transfer.shape[0]
    side = leaf_sends.shape[2]
    per_step = 2
    steps = parents // per_step
    block = 8 * per_step
    bf16 = jnp.bfloat16
    up_leaf, remote, parent_pool = pl.pallas_call(
        functools.partial(upward_kernel, n, steps),
        grid=(steps,),
        out_shape=(
            jax.ShapeDtypeStruct((leaves, rank, rhs), bf16),
            jax.ShapeDtypeStruct((2 * side, rank, rhs), bf16),
            jax.ShapeDtypeStruct((parents + n, rank, rhs), bf16),
        ),
        in_specs=[
            pl.BlockSpec((block, points, rhs), lambda i: (i, 0, 0)),
            pl.BlockSpec((block, rank, points), lambda i: (i, 0, 0)),
            pl.BlockSpec((per_step, 8, rank, rank), lambda i: (i, 0, 0, 0)),
            SMEM,
            SMEM,
        ],
        out_specs=(pl.BlockSpec((block, rank, rhs), lambda i: (i, 0, 0)), ANY, ANY),
        scratch_shapes=[
            pltpu.VMEM((leaves, rank, rhs), bf16),
            pltpu.VMEM((parents, rank, rhs), bf16),
            pltpu.VMEM((2, side, rank, rhs), bf16),
            pltpu.VMEM((n, rank, rhs), bf16),
            pltpu.VMEM((side // CHUNKS, rank, rhs), bf16),
            pltpu.SemaphoreType.DMA((2, CHUNKS)),
            pltpu.SemaphoreType.DMA((2, CHUNKS)),
            pltpu.SemaphoreType.DMA((n,)),
            pltpu.SemaphoreType.DMA((n,)),
            pltpu.SemaphoreType.DMA((3, CHUNKS)),
        ],
        compiler_params=pltpu.CompilerParams(
            collective_id=0, has_side_effects=True, vmem_limit_bytes=40 * 2**20
        ),
        name="upward",
    )(charges, basis_in, transfer, leaf_sends, parent_sends)
    whole = lambda a: pl.BlockSpec(a.shape, lambda i, *_: (0,) * a.ndim)
    return pl.pallas_call(
        downward_kernel,
        out_shape=jax.ShapeDtypeStruct((leaves, points, rhs), bf16),
        grid_spec=pltpu.PrefetchScalarGridSpec(
            num_scalar_prefetch=4,
            grid=(steps,),
            in_specs=[
                whole(leaf_coupling),
                whole(parent_coupling),
                ANY,
                ANY,
                ANY,
                pl.BlockSpec((per_step, 8, rank, rank), lambda i, *_: (i, 0, 0, 0)),
                pl.BlockSpec((block, rank, points), lambda i, *_: (i, 0, 0)),
            ],
            out_specs=pl.BlockSpec((block, points, rhs), lambda i, *_: (i, 0, 0)),
            scratch_shapes=[
                pltpu.VMEM((leaves + 2 * side + 1, rank, rhs), bf16),
                pltpu.VMEM((parents + n + 1, rank, rhs), bf16),
                pltpu.VMEM((rank, leaf_sources.shape[1] * rank), bf16),
                pltpu.VMEM((rank, parent_sources.shape[1] * rank), bf16),
                pltpu.VMEM((parents, rank, rhs), bf16),
                pltpu.SemaphoreType.DMA((3,)),
            ],
        ),
        compiler_params=pltpu.CompilerParams(vmem_limit_bytes=40 * 2**20),
        name="downward",
    )(
        leaf_sources,
        leaf_counts,
        parent_sources,
        parent_counts,
        leaf_coupling,
        parent_coupling,
        up_leaf,
        remote,
        parent_pool,
        transfer,
        basis_out,
    )


def solution(mesh):
    return jax.shard_map(
        functools.partial(shards, mesh.shape["leaf"]),
        mesh=mesh,
        in_specs=(
            P("leaf", None, None),
            P("leaf", None, None),
            P("leaf", None, None),
            P("leaf", None, None, None),
            P(),
            P(),
            P("leaf", None),
            P("leaf"),
            P(),
            P("leaf", None),
            P("leaf"),
            P(),
        ),
        out_specs=P("leaf", None, None),
        check_vma=False,
    )
```

time: 411 us -> 126 us (0.31)
  local copies, waits for them, and re-layouts: 217 us -> 5.26 us
  Pallas kernels: 0 us -> 120 us
  waiting for transfers between devices: 80.4 us -> 0 us
  matrix products: 79.9 us -> 0 us
  other arithmetic: 16.5 us -> 0 us
  starting transfers between devices: 13 us -> 0 us
    gather x12 -> x0, local copies, waits for them, and re-layouts: 203 us -> none  [the longest x9 194 us: one_block(): gathered = extended[redirected]]
    pallas_call x0 -> x2, Pallas kernels: none -> 120 us  [the longest x1 69 us: shards(): pl.pallas_call(functools.partial(upward_kernel, n, steps), grid=(steps,),...]
    all_to_all x1 -> x0, waiting for transfers between devices: 80.4 us -> none  [shards(): lax.all_to_all(up_parent[own_row], 'leaf', split_axis=0, concat_axis=0, t...]
    dot_general x12 -> x0, matrix products: 79.9 us -> none  [the longest x8 47.5 us: one_block(): jnp.einsum('ac,tcr->tar', stacked, flattened, preferred_element_type=jnp....]
    convert_element_type x1 -> x0, local copies, waits for them, and re-layouts: 12 us -> none  [shards(): return jnp.einsum('nkp,nkr->npr', basis_out, leaf_total, preferred_elemen...]
    convert_element_type x1 -> x0, other arithmetic: 7.94 us -> none  [shards(): (leaf_field + pushed.reshape(per_dev, rank_width, rhs_width)).astype(jnp....]
    concatenate x2 -> x0, other arithmetic: 7.17 us -> none  [pooled_product(): jnp.concatenate([pool_rows, jnp.zeros((1, rank_width, rhs_width), pool_ro...]
    all_to_all x1 -> x0, starting transfers between devices: 6.55 us -> none  [shards(): lax.all_to_all(up_parent[own_row], 'leaf', split_axis=0, concat_axis=0, t...]
  transfers between devices with their start and end apart: 3 -> 0, of which waited for: 1 -> 0; matrix products, arithmetic and copies ran while one was open for 9% -> 0% of each run, Pallas kernels for 0% -> 0%
where the time goes in v1:
time: 126 us; the launch traced here: 125 us
  Pallas kernels  120 us (95%)
  local copies, waits for them, and re-layouts  5.26 us (4%)
    pallas_call x1, Pallas kernels, shards(): pl.pallas_call(functools.partial(upward_kernel, n, steps), grid=(steps,),...  69 us
    pallas_call x1, Pallas kernels, shards(): pl.pallas_call(downward_kernel, out_shape=jax.ShapeDtypeStruct((leaves, p...  50.6 us
    unnamed x18, local copies, waits for them, and re-layouts  5.26 us

profile of v1, /device:TPU:1, one launch (start us, length us, event | category | flops | bytes accessed | tf_op | source)
XLA Modules:
  0.0 124.9 jit_solution(1185834237195161173)
XLA Ops:
  0.0 0.8 copy.14.parent_sources
  0.8 0.8 copy.13.leaf_sources
  1.6 0.0 copy-start.1
  1.6 2.2 %copy-done.1 = bf16[256,64,128]{2,1,0:T(8,128)(2,1)S(1)} copy-done((bf16[256,64,128]{2,1,0:T(8,128)(2,1)S(1)}, bf16[256,64,128]{2,1,0:T(8,128)(2,1)}, u32[]{:S(2)}) %copy-start.1) | copy-done | bytes 4194328
  3.8 0.0 copy-start.4
  3.8 0.8 copy-done.4
  4.5 0.0 copy-start.5
  4.5 0.7 copy-done.5
  5.3 0.0 copy-start
  5.3 0.0 copy-start.2
  5.3 0.0 copy-start.3
  5.3 0.0 copy-start.6
  5.3 0.0 copy-start.7
  5.3 69.0 %upward.1 = (bf16[256,64,128]{2,1,0:T(8,128)(2,1)S(1)}, bf16[256,64,128]{2,1,0:T(8,128)(2,1)S(1)}, bf16[64,64,128]{2,1,0:T(8,128)(2,1)S(1)}) custom-call(bf16[256,128,128]{2,1,0:T(8,128)(2,1)} %charges.1, bf16[256,64,128]{2,1,0:T(8,128)(2,1)S(1)} %copy-done.1, bf16[32,8,64,64]{3,2,1,0:T(8,128)(2,1)} %transfer.3, s32[32,2,128]{2,1,0:T(2,128)S(1)} %copy-done.4, ...), custom_call_target="tpu_custom_call" | custom-call | tf_op jit(solution)/shard_map/upward/pallas_call | solution.py:282
  74.3 0.0 copy-done
  74.3 0.0 copy-done.2
  74.3 0.0 copy-done.3
  74.3 0.0 copy-done.6
  74.3 0.0 copy-done.7
  74.3 50.6 %downward.1 = bf16[256,128,128]{2,1,0:T(8,128)(2,1)} custom-call(s32[256,16]{1,0:T(8,128)S(1)} %copy.13.leaf_sources, s32[256]{0:T(256)S(1)} %copy-done.6, s32[32,16]{1,0:T(8,128)S(1)} %copy.14.parent_sources, s32[32]{0:T(128)S(1)} %copy-done.7, bf16[16,64,64]{2,1,0:T(8,128)(2,1)S(1)} %copy-done.2, bf16[16,64,64]{2,1,0:T(8,128)(2,1)S(1)} %copy-done.3, ...), custom_call_target="tpu_custom_call" | custom-call | tf_op jit(solution)/shard_map/downward/pallas_call | solution.py:316
Async XLA Ops:
  1.6 2.2 %copy-start.1 = (bf16[256,64,128]{2,1,0:T(8,128)(2,1)S(1)}, bf16[256,64,128]{2,1,0:T(8,128)(2,1)}, u32[]{:S(2)}) copy-start(bf16[256,64,128]{2,1,0:T(8,128)(2,1)} %basis_in.1) | copy-start | bytes 12582916
  3.8 0.8 copy-start.4
  4.5 0.7 copy-start.5
  5.3 69.0 %copy-start = (bf16[32,8,64,64]{3,2,1,0:T(8,128)(2,1)S(1)}, bf16[32,8,64,64]{3,2,1,0:T(8,128)(2,1)}, u32[]{:S(2)}) copy-start(bf16[32,8,64,64]{3,2,1,0:T(8,128)(2,1)} %transfer.3) | copy-start | bytes 6291460
  5.3 69.0 %copy-start.2 = (bf16[16,64,64]{2,1,0:T(8,128)(2,1)S(1)}, bf16[16,64,64]{2,1,0:T(8,128)(2,1)}, u32[]{:S(2)}) copy-start(bf16[16,64,64]{2,1,0:T(8,128)(2,1)} %leaf_coupling.1) | copy-start | bytes 393220
  5.3 69.0 %copy-start.3 = (bf16[16,64,64]{2,1,0:T(8,128)(2,1)S(1)}, bf16[16,64,64]{2,1,0:T(8,128)(2,1)}, u32[]{:S(2)}) copy-start(bf16[16,64,64]{2,1,0:T(8,128)(2,1)} %parent_coupling.1) | copy-start | bytes 393220
  5.3 69.0 %copy-start.6 = (s32[256]{0:T(256)S(1)}, s32[256]{0:T(256)}, u32[]{:S(2)}) copy-start(s32[256]{0:T(256)} %leaf_counts.1) | copy-start | bytes 3076
  5.3 69.1 %copy-start.7 = (s32[32]{0:T(128)S(1)}, s32[32]{0:T(128)}, u32[]{:S(2)}) copy-start(s32[32]{0:T(128)} %parent_counts.1) | copy-start | bytes 388

commit v2 on v0

v2 whole, which is shorter than its diff:
```python
import functools

import jax
import jax.numpy as jnp
from jax import lax
from jax.experimental import pallas as pl
from jax.experimental.pallas import tpu as pltpu
from jax.sharding import PartitionSpec as P

CHUNKS = 4
LOADS = 8
GROUP = 4
CODE = 1024
ANY = pl.BlockSpec(memory_space=pl.ANY)
SMEM = pl.BlockSpec(memory_space=pltpu.SMEM)
VMEM = pl.BlockSpec(memory_space=pltpu.VMEM)
CONTRACT_FIRST = (((0,), (0,)), ((), ()))
MESH = pl.DeviceIdType.MESH


def field_pair(first, second, pool, slots, stacked):
    columns = [
        jnp.concatenate([pool[slots[j, target]] for j in range(slots.shape[0])], 0) for target in (first, second)
    ]
    return jnp.dot(stacked[...], jnp.concatenate(columns, 1), preferred_element_type=jnp.float32)


def upward_kernel(
    n,
    charges_hbm,
    basis_hbm,
    transfer_hbm,
    leaf_sends,
    parent_sends,
    near_slots,
    parent_slots,
    far_codes,
    leaf_coupling,
    parent_coupling,
    far_out,
    field_out,
    list_out,
    charges,
    basis_in,
    transfer,
    up_all,
    near,
    far_stage,
    fast_stage,
    parent_all,
    parent_stage,
    parent_pool,
    down,
    field,
    stacked,
    pstacked,
    zeros,
    load_sem,
    far_sem,
    fast_sem,
    parent_send_sem,
    parent_recv_sem,
    zero_sem,
    field_sem,
):
    me = lax.axis_index("leaf")
    odd = lax.rem(me, 2)
    fast_target = me + 1 - 2 * odd
    far_target = me - 1 + 2 * odd
    has_far = jnp.logical_and(far_target >= 0, far_target < n)
    leaves, rank, rhs = up_all.shape
    parents = parent_all.shape[0]
    side = far_stage.shape[0]
    piece = side // CHUNKS
    part = leaves // LOADS
    bf16 = up_all.dtype

    loads = [pltpu.make_async_copy(transfer_hbm, transfer, load_sem.at[2, 0])]
    for c in range(LOADS):
        rows = pl.ds(c * part, part)
        loads.append(pltpu.make_async_copy(basis_hbm.at[rows], basis_in.at[rows], load_sem.at[0, c]))
        loads.append(pltpu.make_async_copy(charges_hbm.at[rows], charges.at[rows], load_sem.at[1, c]))
    for load in loads[1:] + loads[:1]:
        load.start()

    barrier = pltpu.get_barrier_semaphore()

    def greet(k, carry):
        pl.semaphore_signal(barrier, inc=1, device_id=(lax.rem(me + k, n),), device_id_type=MESH)
        return carry

    lax.fori_loop(1, n, greet, 0)
    near[leaves + side] = jnp.zeros((rank, rhs), bf16)
    parent_pool[parents + n] = jnp.zeros((rank, rhs), bf16)
    zeros[...] = jnp.zeros_like(zeros)
    for j in range(leaf_coupling.shape[0]):
        stacked[:, j * rank : (j + 1) * rank] = leaf_coupling[j]
    for j in range(parent_coupling.shape[0]):
        pstacked[:, j * rank : (j + 1) * rank] = parent_coupling[j]
    for load in loads[1:]:
        load.wait()
    pl.semaphore_wait(barrier, n - 1)

    def up(leaf):
        return jnp.dot(basis_in[leaf], charges[leaf], preferred_element_type=jnp.float32).astype(bf16)

    def far_copy(c):
        rows = pl.ds(c * piece, piece)
        return pltpu.make_async_remote_copy(
            src_ref=far_stage.at[rows],
            dst_ref=far_out.at[rows],
            send_sem=far_sem.at[0, c],
            recv_sem=far_sem.at[1, c],
            device_id=(far_target,),
            device_id_type=MESH,
        )

    def zero_copy(c):
        return pltpu.make_async_copy(zeros, far_out.at[pl.ds(c * piece, piece)], zero_sem.at[c])

    for c in range(CHUNKS):

        def fill_far(i, carry):
            far_stage[c * piece + i] = up(leaf_sends[me, odd, c * piece + i])
            return carry

        lax.fori_loop(0, piece, fill_far, 0, unroll=8)

        @pl.when(has_far)
        def _():
            far_copy(c).start()

        @pl.when(jnp.logical_not(has_far))
        def _():
            zero_copy(c).start()

    def up_row(leaf, carry):
        row = up(leaf)
        up_all[leaf] = row
        near[leaf] = row
        return carry

    lax.fori_loop(0, leaves, up_row, 0, unroll=8)
    loads[0].wait()

    def up_parent(p, carry):
        row = lax.dot_general(
            transfer[p].reshape(8 * rank, rank),
            up_all[pl.ds(8 * p, 8)].reshape(8 * rank, rhs),
            CONTRACT_FIRST,
            preferred_element_type=jnp.float32,
        ).astype(bf16)
        parent_all[p] = row
        parent_pool[p] = row
        return carry

    lax.fori_loop(0, parents, up_parent, 0, unroll=2)

    def fill_parent(d, carry):
        parent_stage[d] = parent_all[parent_sends[me, d]]
        return carry

    lax.fori_loop(0, n, fill_parent, 0)

    def parent_copy(k):
        target = lax.rem(me + k, n)
        return pltpu.make_async_remote_copy(
            src_ref=parent_stage.at[target],
            dst_ref=parent_pool.at[parents + me],
            send_sem=parent_send_sem.at[k],
            recv_sem=parent_recv_sem.at[k],
            device_id=(target,),
            device_id_type=MESH,
        )

    def start_parent(k, carry):
        parent_copy(k).start()
        return carry

    lax.fori_loop(1, n, start_parent, 0)
    parent_pool[parents + me] = parent_stage[me]

    def fill_fast(i, carry):
        fast_stage[i] = up_all[leaf_sends[me, 1 - odd, i]]
        return carry

    lax.fori_loop(0, side, fill_fast, 0, unroll=4)
    fast_copy = pltpu.make_async_remote_copy(
        src_ref=fast_stage,
        dst_ref=near.at[pl.ds(leaves, side)],
        send_sem=fast_sem.at[0],
        recv_sem=fast_sem.at[1],
        device_id=(fast_target,),
        device_id_type=MESH,
    )
    fast_copy.start()

    width = far_codes.shape[0]
    codes = [far_codes[j : j + 1, :] for j in range(width)]
    used = [code >= 0 for code in codes]
    place = jnp.zeros_like(codes[0])
    places = []
    for j in range(width):
        places.append(place)
        place = place + used[j].astype(jnp.int32)
    for p in range(width):
        entry = jnp.full_like(place, side)
        for j in range(p, width):
            entry = jnp.where(jnp.logical_and(used[j], places[j] == p), codes[j], entry)
        list_out[p : p + 1, :] = entry
    list_out[width : width + 1, :] = place

    fast_copy.wait()

    def near_pair(i, carry):
        pair = field_pair(2 * i, 2 * i + 1, near, near_slots, stacked)
        field[2 * i] = pair[:, :rhs]
        field[2 * i + 1] = pair[:, rhs:]
        return carry

    lax.fori_loop(0, leaves // 2, near_pair, 0, unroll=2)

    def wait_parent(k, carry):
        source = lax.rem(me - k + n, n)
        copy = pltpu.make_async_remote_copy(
            src_ref=parent_stage.at[lax.rem(me + k, n)],
            dst_ref=parent_pool.at[parents + source],
            send_sem=parent_send_sem.at[k],
            recv_sem=parent_recv_sem.at[k],
            device_id=(lax.rem(me + k, n),),
            device_id_type=MESH,
        )
        copy.wait_send()
        copy.wait_recv()
        return carry

    lax.fori_loop(1, n, wait_parent, 0)

    def parent_pair(i, carry):
        pair = field_pair(2 * i, 2 * i + 1, parent_pool, parent_slots, pstacked)
        down[2 * i] = pair[:, :rhs].astype(bf16)
        down[2 * i + 1] = pair[:, rhs:].astype(bf16)
        return carry

    lax.fori_loop(0, parents // 2, parent_pair, 0)

    def field_copy(c):
        rows = pl.ds(c * part, part)
        return pltpu.make_async_copy(field.at[rows], field_out.at[rows], field_sem.at[c])

    for c in range(LOADS):

        def push(i, carry):
            p = c * (parents // LOADS) + i
            pushed = jnp.dot(transfer[p].reshape(8 * rank, rank), down[p], preferred_element_type=jnp.float32)
            rows = pl.ds(8 * p, 8)
            field[rows] = field[rows] + pushed.reshape(8, rank, rhs)
            return carry

        lax.fori_loop(0, parents // LOADS, push, 0, unroll=2)
        field_copy(c).start()
    for c in range(LOADS):
        field_copy(c).wait()
    for c in range(CHUNKS):

        @pl.when(has_far)
        def _():
            far_copy(c).wait()

        @pl.when(jnp.logical_not(has_far))
        def _():
            zero_copy(c).wait()


def downward_kernel(lists, leaf_coupling, far, field, basis_out, potential, pool, even_side, odd_side, total, sem):
    step = pl.program_id(0)
    block, rank, rhs = total.shape
    side = far.shape[0]
    width = leaf_coupling.shape[0]

    @pl.when(step == 0)
    def _():
        copy = pltpu.make_async_copy(far, pool.at[pl.ds(0, side)], sem)
        copy.start()
        pool[side] = jnp.zeros((rank, rhs), pool.dtype)
        blank = jnp.zeros((rank, rank), pool.dtype)
        for j in range(width):
            even_side[j] = jnp.concatenate([leaf_coupling[j], blank], 1)
            odd_side[j] = jnp.concatenate([blank, leaf_coupling[j]], 1)
        copy.wait()

    def group(target, g):
        codes = [lists[GROUP * g + k, target] for k in range(GROUP)]
        slot = [lax.shift_right_logical(code, 10) for code in codes]
        left = [even_side[slot[k]] + odd_side[slot[k + 1]] for k in range(0, GROUP, 2)]
        rows = [pool[jnp.bitwise_and(code, CODE - 1)] for code in codes]
        return jnp.dot(jnp.concatenate(left, 1), jnp.concatenate(rows, 0), preferred_element_type=jnp.float32)

    for leaf in range(block):
        total[leaf] = field[leaf] + group(step * block + leaf, 0)

    def rest(leaf, carry):
        target = step * block + leaf
        groups = lax.shift_right_logical(lists[width, target] + (GROUP - 1), 2)

        def more(g, inner):
            total[leaf] += group(target, g)
            return inner

        lax.fori_loop(1, groups, more, 0)
        return carry

    lax.fori_loop(0, block, rest, 0)
    for leaf in range(block):
        potential[leaf] = lax.dot_general(
            basis_out[leaf], total[leaf].astype(jnp.bfloat16), CONTRACT_FIRST, preferred_element_type=jnp.float32
        ).astype(potential.dtype)


def shards(
    n,
    charges,
    basis_in,
    basis_out,
    transfer,
    leaf_coupling,
    parent_coupling,
    leaf_sources,
    leaf_counts,
    leaf_sends,
    parent_sources,
    parent_counts,
    parent_sends,
):
    leaves, points, rhs = charges.shape
    rank = basis_in.shape[1]
    parents = transfer.shape[0]
    side = leaf_sends.shape[2]
    width = leaf_sources.shape[1]
    pwidth = parent_sources.shape[1]
    block = 16
    bf16 = jnp.bfloat16
    odd = lax.rem(lax.axis_index("leaf"), 2)
    sources = leaf_sources.T
    slot = lax.broadcasted_iota(jnp.int32, sources.shape, 0)
    valid = slot < leaf_counts[None, :]
    fast_row = sources - (leaves + (1 - odd) * side)
    far_row = sources - (leaves + odd * side)
    in_fast = (fast_row >= 0) & (fast_row < side)
    in_far = (far_row >= 0) & (far_row < side)
    near_row = jnp.where(sources < leaves, sources, jnp.where(in_fast, leaves + fast_row, leaves + side))
    near_slots = jnp.where(valid, near_row, leaves + side)
    far_codes = jnp.where(valid & in_far & (sources >= leaves), slot * CODE + far_row, -1)
    psources = parent_sources.T
    pslot = lax.broadcasted_iota(jnp.int32, psources.shape, 0)
    parent_slots = jnp.where(pslot < parent_counts[None, :], psources, parents + n)
    list_rows = width + 8
    far, field, lists = pl.pallas_call(
        functools.partial(upward_kernel, n),
        out_shape=(
            jax.ShapeDtypeStruct((side, rank, rhs), bf16),
            jax.ShapeDtypeStruct((leaves, rank, rhs), jnp.float32),
            jax.ShapeDtypeStruct((list_rows, leaves), jnp.int32),
        ),
        in_specs=[ANY, ANY, ANY, SMEM, SMEM, SMEM, SMEM, VMEM, VMEM, VMEM],
        out_specs=(ANY, ANY, VMEM),
        scratch_shapes=[
            pltpu.VMEM((leaves, points, rhs), bf16),
            pltpu.VMEM((leaves, rank, points), bf16),
            pltpu.VMEM((parents, 8, rank, rank), bf16),
            pltpu.VMEM((leaves, rank, rhs), bf16),
            pltpu.VMEM((leaves + side + 1, rank, rhs), bf16),
            pltpu.VMEM((side, rank, rhs), bf16),
            pltpu.VMEM((side, rank, rhs), bf16),
            pltpu.VMEM((parents, rank, rhs), bf16),
            pltpu.VMEM((n, rank, rhs), bf16),
            pltpu.VMEM((parents + n + 1, rank, rhs), bf16),
            pltpu.VMEM((parents, rank, rhs), bf16),
            pltpu.VMEM((leaves, rank, rhs), jnp.float32),
            pltpu.VMEM((rank, width * rank), bf16),
            pltpu.VMEM((rank, pwidth * rank), bf16),
            pltpu.VMEM((side // CHUNKS, rank, rhs), bf16),
            pltpu.SemaphoreType.DMA((3, LOADS)),
            pltpu.SemaphoreType.DMA((2, CHUNKS)),
            pltpu.SemaphoreType.DMA((2,)),
            pltpu.SemaphoreType.DMA((n,)),
            pltpu.SemaphoreType.DMA((n,)),
            pltpu.SemaphoreType.DMA((CHUNKS,)),
            pltpu.SemaphoreType.DMA((LOADS,)),
        ],
        compiler_params=pltpu.CompilerParams(
            collective_id=0, has_side_effects=True, vmem_limit_bytes=56 * 2**20
        ),
        name="upward",
    )(
        charges,
        basis_in,
        transfer,
        leaf_sends,
        parent_sends,
        near_slots,
        parent_slots,
        far_codes,
        leaf_coupling,
        parent_coupling,
    )
    return pl.pallas_call(
        downward_kernel,
        out_shape=jax.ShapeDtypeStruct((leaves, points, rhs), bf16),
        grid_spec=pltpu.PrefetchScalarGridSpec(
            num_scalar_prefetch=1,
            grid=(leaves // block,),
            in_specs=[
                pl.BlockSpec(leaf_coupling.shape, lambda i, *_: (0, 0, 0)),
                ANY,
                pl.BlockSpec((block, rank, rhs), lambda i, *_: (i, 0, 0)),
                pl.BlockSpec((block, rank, points), lambda i, *_: (i, 0, 0)),
            ],
            out_specs=pl.BlockSpec((block, points, rhs), lambda i, *_: (i, 0, 0)),
            scratch_shapes=[
                pltpu.VMEM((side + 1, rank, rhs), bf16),
                pltpu.VMEM((width, rank, 2 * rank), bf16),
                pltpu.VMEM((width, rank, 2 * rank), bf16),
                pltpu.VMEM((block, rank, rhs), jnp.float32),
                pltpu.SemaphoreType.DMA,
            ],
        ),
        compiler_params=pltpu.CompilerParams(vmem_limit_bytes=60 * 2**20),
        name="downward",
    )(lists, leaf_coupling, far, field, basis_out)


def solution(mesh):
    return jax.shard_map(
        functools.partial(shards, mesh.shape["leaf"]),
        mesh=mesh,
        in_specs=(
            P("leaf", None, None),
            P("leaf", None, None),
            P("leaf", None, None),
            P("leaf", None, None, None),
            P(),
            P(),
            P("leaf", None),
            P("leaf"),
            P(),
            P("leaf", None),
            P("leaf"),
            P(),
        ),
        out_specs=P("leaf", None, None),
        check_vma=False,
    )
```

time: 411 us -> 99.8 us (0.24)
  local copies, waits for them, and re-layouts: 217 us -> 0 us
  Pallas kernels: 0 us -> 95.6 us
  waiting for transfers between devices: 80.4 us -> 0 us
  matrix products: 79.9 us -> 0 us
  other arithmetic: 16.5 us -> 2.7 us
  starting transfers between devices: 13 us -> 0 us
    gather x12 -> x0, local copies, waits for them, and re-layouts: 203 us -> none  [the longest x9 194 us: one_block(): gathered = extended[redirected]]
    pallas_call x0 -> x2, Pallas kernels: none -> 95.6 us  [the longest x1 70.7 us: shards(): pl.pallas_call(functools.partial(upward_kernel, n), out_shape=(jax.ShapeD...]
    all_to_all x1 -> x0, waiting for transfers between devices: 80.4 us -> none  [shards(): lax.all_to_all(up_parent[own_row], 'leaf', split_axis=0, concat_axis=0, t...]
    dot_general x12 -> x0, matrix products: 79.9 us -> none  [the longest x8 47.5 us: one_block(): jnp.einsum('ac,tcr->tar', stacked, flattened, preferred_element_type=jnp....]
    convert_element_type x1 -> x0, local copies, waits for them, and re-layouts: 12 us -> none  [shards(): return jnp.einsum('nkp,nkr->npr', basis_out, leaf_total, preferred_elemen...]
    convert_element_type x1 -> x0, other arithmetic: 7.94 us -> none  [shards(): (leaf_field + pushed.reshape(per_dev, rank_width, rhs_width)).astype(jnp....]
    concatenate x2 -> x0, other arithmetic: 7.17 us -> none  [pooled_product(): jnp.concatenate([pool_rows, jnp.zeros((1, rank_width, rhs_width), pool_ro...]
    all_to_all x1 -> x0, starting transfers between devices: 6.55 us -> none  [shards(): lax.all_to_all(up_parent[own_row], 'leaf', split_axis=0, concat_axis=0, t...]
  transfers between devices with their start and end apart: 3 -> 0, of which waited for: 1 -> 0; matrix products, arithmetic and copies ran while one was open for 9% -> 0% of each run, Pallas kernels for 0% -> 0%
where the time goes in v2:
time: 99.8 us; the launch traced here: 98.3 us
  Pallas kernels  95.6 us (96%)
  other arithmetic  2.7 us (3%)
    pallas_call x1, Pallas kernels, shards(): pl.pallas_call(functools.partial(upward_kernel, n), out_shape=(jax.ShapeD...  70.7 us
    pallas_call x1, Pallas kernels, shards(): pl.pallas_call(downward_kernel, out_shape=jax.ShapeDtypeStruct((leaves, p...  24.9 us

profile of v2, /device:TPU:1, one launch (start us, length us, event | category | flops | bytes accessed | tf_op | source)
XLA Modules:
  0.0 98.3 jit_solution(11870293790272464029)
XLA Ops:
  0.0 1.3 %bitcast_select_fusion.parent_slots = s32[16,32]{1,0:T(8,128)} fusion(s32[32,16]{0,1:T(8,128)} %param.21, s32[32]{0:T(128)} %param.22), kind=kLoop, calls=%fused_computation.11 | loop fusion | flops 1024 | bytes 4224 | tf_op jit(solution)/shard_map/jit(_where)/select_n | solution.py:356
  1.3 1.4 %add_select_fusion = (s32[16,256]{1,0:T(8,128)}, s32[16,256]{1,0:T(8,128)}) fusion(s32[256,16]{0,1:T(8,128)} %param.18, s32[16]{0:T(128)S(1)} %iota_multiply_fusion, s32[]{:T(128)S(6)} %add.14, s32[256]{0:T(256)} %param.19, s32[]{:T(128)S(6)} %add.12), kind=kLoop, calls=%fused_computation.5 | loop fusion | flops 77824 | bytes 50248 | tf_op jit(solution)/shard_map/jit(_where)/select_n | solution.py:353
  2.7 70.7 %upward.1 = (bf16[128,64,128]{2,1,0:T(8,128)(2,1)}, f32[256,64,128]{2,1,0:T(8,128)}, s32[24,256]{1,0:T(8,128)}) custom-call(bf16[256,128,128]{2,1,0:T(8,128)(2,1)} %charges_hbm.1, bf16[256,64,128]{2,1,0:T(8,128)(2,1)} %basis_hbm.1, bf16[32,8,64,64]{3,2,1,0:T(8,128)(2,1)} %transfer_hbm.1, s32[32,2,128]{2,1,0:T(2,128)} %leaf_sends.1, s32[32,32]{1,0:T(8,128)} %parent_sends.1, ...), custom_call_target="tpu_custom_call" | custom-call | tf_op jit(solution)/shard_map/upward/pallas_call | solution.py:358
  73.4 24.9 %downward.1 = bf16[256,128,128]{2,1,0:T(8,128)(2,1)} custom-call(s32[24,256]{1,0:T(8,128)} %get-tuple-element.8.lists, bf16[16,64,64]{2,1,0:T(8,128)(2,1)} %leaf_coupling.3, bf16[128,64,128]{2,1,0:T(8,128)(2,1)} %get-tuple-element.9.far, f32[256,64,128]{2,1,0:T(8,128)} %get-tuple-element.10.field, bf16[256,64,128]{2,1,0:T(8,128)(2,1)} %basis_out.1), custom_call_target="tpu_custom_call" | custom-call | tf_op jit(solution)/shard_map/downward/pallas_call | solution.py:407
  (1 shorter events, 0.0 us)
